TPU v7x, 32 devices: a whole 2x2x4 slice. The times are simulated.
32 devices in a mesh: group: 4 (over y, x), sub: 8 (over z, core).
Axes of the slice: x: 2, y: 2, z: 4, core: 2. Of those that a mesh axis runs over, the one named last changes fastest.
Arguments:
- points: float32 [3, 262144], P(None, ('group', 'sub')), as said below
- probes: float32 [32, 262144], P(None, ('group', 'sub')), may hold values from -6 to 6
- morton: int32 [262144], P(('group', 'sub')), may hold values from 0 to 8191, as said below
- near_list: int32 [2048, 27], P(('group', 'sub')), may hold values from -1 to 2047, as said below
- leaf_far: int32 [2048, 24], P(('group', 'sub')), may hold values from -1 to 2047, as said below
- box_far: int32 [256, 4], P(('group', 'sub')), may hold values from -1 to 255, as said below
- subtree_far: int32 [32, 4], P(('group', 'sub')), may hold values from -1 to 31, as said below
- leaf_skeleton: float32 [2048, 3, 64], P(('group', 'sub')), as said below
- box_skeleton: float32 [256, 3, 128], P(('group', 'sub')), as said below
- subtree_skeleton: float32 [32, 3, 256], P(('group', 'sub')), as said below
- group_skeleton: float32 [4, 3, 256], replicated, as said below
- leaf_basis: float32 [2048, 64, 128], P(('group', 'sub')), may hold values from -0.5 to 0.5
- leaf_transfer: float32 [2048, 64, 128], P(('group', 'sub')), may hold values from -0.25 to 0.25
- box_transfer: float32 [256, 128, 256], P(('group', 'sub')), may hold values from -0.1875 to 0.1875
- subtree_transfer: float32 [32, 256, 256], P(('group', 'sub')), may hold values from -0.375 to 0.375
Outputs:
- kernel_product: float32 [32, 262144], P(None, ('group', 'sub'))
Inputs may be any that keep to these rules, and one draw needn't show every extreme that they name: `morton`: each block of 8192 entries is a permutation of 0 to 8191. `near_list`: row l starts with l, then distinct leaves within 32 of l; -1 marks an empty slot. `leaf_far`: row l holds distinct leaves within 32 of l, none in its near list; -1 marks an empty slot. `box_far`: row b holds distinct other boxes of the same subtree; -1 marks an empty slot. `subtree_far`: row c holds distinct other subtrees of the same group; -1 marks an empty slot. `points`: coordinates in leaf-cell units. `leaf_skeleton`: coordinates in leaf-cell units. `box_skeleton`: coordinates in leaf-cell units. `subtree_skeleton`: coordinates in leaf-cell units. `group_skeleton`: coordinates in leaf-cell units.
All inputs are finite; a program needn't handle non-finite values.
Results may differ from a plain program's by a relative error of at most 0.0003.
Values sent between devices are 32-bit elements; how exact they have to be, the bound alone decides.
A program may use at most 128 MiB of HBM per device.

v0:
```python
import math

import jax
import jax.numpy as jnp
from jax import lax
from jax.sharding import PartitionSpec as P

P_SIZE = 128
CH = 8
NEAR = 27
HALO = 32


highest = lax.Precision.HIGHEST
matern_rate = math.sqrt(3.0) / 12.0


def with_halo(cells, sides, width):
    for axis, dim in sides:
        count = lax.axis_size(axis)
        ends = count - 1
        head = lax.slice_in_dim(cells, 0, width, axis=dim)
        tail = lax.slice_in_dim(cells, cells.shape[dim] - width, cells.shape[dim], axis=dim)
        cells = jnp.concatenate(
            [
                lax.ppermute(tail, axis, [(i, (i + 1) % count) for i in range(ends)]),
                cells,
                lax.ppermute(head, axis, [((i + 1) % count, i) for i in range(ends)]),
            ],
            axis=dim,
        )
    return cells


def matern(source, target):
    squared = None
    for coord_id in range(3):
        offset = source[..., coord_id, :, None] - target[..., coord_id, None, :]
        squared = offset * offset if coord_id == 0 else squared + offset * offset
    radius = jnp.sqrt(squared + 0.0001) * matern_rate
    return (1.0 + radius) * jnp.exp(-radius)


def body(
    points,
    probes,
    morton,
    near_list,
    leaf_far,
    box_far,
    subtree_far,
    leaf_skeleton,
    box_skeleton,
    subtree_skeleton,
    group_skeleton,
    leaf_basis,
    leaf_transfer,
    box_transfer,
    subtree_transfer,
):
    leaf_count = near_list.shape[0]
    point_count = points.shape[1]
    probe_count = probes.shape[0]
    box_count = box_far.shape[0]
    subtree_count = subtree_far.shape[0]
    rank_leaf = leaf_basis.shape[1]
    rank_box = box_transfer.shape[1]
    rank_subtree = subtree_transfer.shape[1]
    rank_group = subtree_transfer.shape[2]
    device = lax.axis_index(("group", "sub"))
    leaf_points = points[:, morton].reshape(3, leaf_count, P_SIZE).transpose(1, 0, 2)
    leaf_probes = probes[:, morton].reshape(probe_count, leaf_count, P_SIZE).transpose(1, 0, 2)
    coef_leaf = jnp.einsum("lvp,lrp->lvr", leaf_probes, leaf_basis, precision=highest)
    point_width = 3 * P_SIZE
    probe_width = probe_count * P_SIZE
    skel_width = 3 * rank_leaf
    geometry = jnp.concatenate(
        [
            leaf_points.reshape(leaf_count, -1),
            leaf_probes.reshape(leaf_count, -1),
            leaf_skeleton.reshape(leaf_count, -1),
        ],
        axis=1,
    )
    extended = with_halo(geometry, ((("group", "sub"), 0),), HALO)
    ext_coef = with_halo(coef_leaf.reshape(leaf_count, -1), ((("group", "sub"), 0),), HALO).reshape(
        -1, probe_count, rank_leaf
    )
    ext_points = extended[:, :point_width].reshape(-1, 3, P_SIZE)
    ext_probes = extended[:, point_width : point_width + probe_width].reshape(
        -1, probe_count, P_SIZE
    )
    ext_skeleton = extended[
        :, point_width + probe_width : point_width + probe_width + skel_width
    ].reshape(-1, 3, rank_leaf)
    base_leaf = device * leaf_count - HALO

    def slot_sum(anchor_sets, partner_ids, partner_sets, partner_values, factor):
        usable = partner_ids >= 0
        local_ids = jnp.where(usable, partner_ids - base_leaf, 0)

        def add_slot(summed, slot):
            slot_ids, slot_mask = slot
            kernel_tiles = matern(anchor_sets, partner_sets[slot_ids]) * slot_mask[:, None, None]
            return (
                summed
                + jnp.einsum(
                    "lab,lvb->lva", kernel_tiles, partner_values[slot_ids], precision=highest
                ),
                None,
            )

        initial = jnp.zeros(
            (anchor_sets.shape[0], partner_values.shape[1], anchor_sets.shape[2]), jnp.float32
        )
        summed, unused = lax.scan(add_slot, initial, (local_ids.T, usable.T.astype(jnp.float32)))
        return summed * factor

    near_field = slot_sum(leaf_points, near_list, ext_points, ext_probes, (P_SIZE * NEAR) ** (-0.5))
    local_leaf = slot_sum(
        leaf_skeleton, leaf_far, ext_skeleton, ext_coef, (rank_leaf * leaf_far.shape[1]) ** (-0.5)
    )
    coef_box = (
        jnp.einsum("lvr,lrs->lvs", coef_leaf, leaf_transfer, precision=highest)
        .reshape(box_count, CH, probe_count, rank_box)
        .sum(axis=1)
    )
    box_usable = box_far >= 0
    box_safe = jnp.where(box_usable, box_far - device * box_count, 0)
    box_tiles = (
        matern(box_skeleton[:, None], box_skeleton[box_safe])
        * box_usable.astype(jnp.float32)[:, :, None, None]
    )
    local_box = jnp.einsum("bjrs,bjvs->bvr", box_tiles, coef_box[box_safe], precision=highest) * (
        rank_box * box_far.shape[1]
    ) ** (-0.5)
    coef_subtree = (
        jnp.einsum("bvr,brs->bvs", coef_box, box_transfer, precision=highest)
        .reshape(subtree_count, CH, probe_count, rank_subtree)
        .sum(axis=1)
    )
    group_index = lax.axis_index("group")
    group_boxes = lax.axis_size("sub") * subtree_count
    subtree_usable = subtree_far >= 0
    subtree_ids = subtree_far - group_index * group_boxes
    coef_width = probe_count * rank_subtree
    packed_subtree = jnp.concatenate(
        [coef_subtree.reshape(subtree_count, -1), subtree_skeleton.reshape(subtree_count, -1)],
        axis=1,
    )
    subtree_start = jnp.zeros((subtree_count, probe_count, rank_subtree), jnp.float32)
    segment = lax.all_gather(packed_subtree, "sub", axis=0, tiled=True)
    row_count = segment.shape[0]
    segment_coef = segment[:, :coef_width].reshape(row_count, probe_count, rank_subtree)
    segment_skel = segment[:, coef_width:].reshape(row_count, 3, rank_subtree)
    matches = (
        subtree_ids[:, :, None] == jnp.arange(row_count, dtype=jnp.int32)[None, None, :]
    ) & subtree_usable[:, :, None]
    weights = jnp.sum(matches.astype(jnp.float32), axis=1)

    def add_source(running, source):
        source_skel, source_coef, source_weight = source
        kernel_tiles = matern(subtree_skeleton, source_skel[None]) * source_weight[:, None, None]
        return (
            running + jnp.einsum("crs,vs->cvr", kernel_tiles, source_coef, precision=highest),
            None,
        )

    running, unused = lax.scan(add_source, subtree_start, (segment_skel, segment_coef, weights.T))
    local_subtree = running * (rank_subtree * subtree_far.shape[1]) ** (-0.5)
    partial_group = jnp.einsum("cvr,crs->vs", coef_subtree, subtree_transfer, precision=highest)
    group_count = group_skeleton.shape[0]
    group_total = lax.psum(partial_group, "sub")
    coef_group = lax.all_gather(group_total[None], "group", axis=0, tiled=True)
    own_skel = lax.dynamic_index_in_dim(group_skeleton, group_index, 0, keepdims=False)
    other_mask = (jnp.arange(group_count, dtype=jnp.int32) != group_index).astype(jnp.float32)
    group_tiles = matern(own_skel[None], group_skeleton) * other_mask[:, None, None]
    local_group = jnp.einsum(
        "hrs,hvs->vr", group_tiles, coef_group, precision=highest
    ) * rank_group ** (-0.5)
    down_subtree = local_subtree + jnp.einsum(
        "vs,crs->cvr", local_group, subtree_transfer, precision=highest
    )
    down_box = local_box + jnp.einsum(
        "bvs,brs->bvr", jnp.repeat(down_subtree, CH, axis=0), box_transfer, precision=highest
    )
    down_leaf = local_leaf + jnp.einsum(
        "lvs,lrs->lvr", jnp.repeat(down_box, CH, axis=0), leaf_transfer, precision=highest
    )
    result = near_field + jnp.einsum("lvr,lrp->lvp", down_leaf, leaf_basis, precision=highest)
    ordered = result.transpose(1, 0, 2).reshape(probe_count, point_count)
    return jnp.zeros_like(ordered).at[:, morton].set(ordered)


def solution(mesh):
    placed = (
        P(None, ("group", "sub")),
        P(None, ("group", "sub")),
        P(("group", "sub")),
        P(("group", "sub"), None),
        P(("group", "sub"), None),
        P(("group", "sub"), None),
        P(("group", "sub"), None),
        P(("group", "sub"), None, None),
        P(("group", "sub"), None, None),
        P(("group", "sub"), None, None),
        P(),
        P(("group", "sub"), None, None),
        P(("group", "sub"), None, None),
        P(("group", "sub"), None, None),
        P(("group", "sub"), None, None),
    )
    return jax.shard_map(
        body, mesh=mesh, in_specs=placed, out_specs=P(None, ("group", "sub")), check_vma=False
    )
```

profile of v0, /device:TPU:1, one launch (start us, length us, event | category | flops | bytes accessed | tf_op | source)
XLA Modules:
  0.0 1096.9 jit_solution(3002730051434759015)
XLA Ops:
  5.1 29.9 %gather_fusion.5 = f32[8192,32]{1,0:T(8,128)} fusion(f32[32,8192]{0,1:T(8,128)} %copy.84, s32[8192]{0:T(1024)S(1)} %get-tuple-element.322), kind=kCustom, calls=%fused_computation.5 | custom fusion | bytes 2129920 | tf_op jit(solution)/shard_map/gather | solution.py:72
  58.3 29.9 %gather_fusion.4 = f32[8192,3]{1,0:T(8,128)} fusion(f32[3,8192]{0,1:T(8,128)} %copy.81, s32[8192]{0:T(1024)S(1)} %get-tuple-element.322), kind=kCustom, calls=%fused_computation.4 | custom fusion | bytes 229376 | tf_op jit(solution)/shard_map/gather | solution.py:71
  118.7 20.2 %all-gather = f32[8,1,8960]{2,1,0:T(1,128)S(1)} all-gather(f32[1,1,8960]{2,1,0:T(1,128)S(1)} %maximum_bitcast_fusion), channel_id=1, replica_groups=mesh['group'=4,'sub'=8] {'sub'}, dimensions={0}, use_global_device_ids=true | all-gather | bytes 322560 | tf_op jit(solution)/shard_map/all_gather | solution.py:152
  153.7 22.5 %psum.7 = f32[1,32,256]{2,1,0:T(8,128)S(1)} all-reduce(f32[1,32,256]{2,1,0:T(8,128)S(1)} %convolution_bitcast_fusion.3), channel_id=1, replica_groups=mesh['group'=4,'sub'=8] {'sub'}, use_global_device_ids=true, to_apply=%region_8.9 | all-reduce | flops 8192 | bytes 65536 | tf_op jit(solution)/shard_map/psum | solution.py:173
  176.2 8.2 all_gather.7
  185.2 33.4 %while.35 = (s32[]{:T(128)}, f32[1,32,256]{2,1,0:T(8,128)}, f32[8,32,256]{2,0,1:T(8,128)}, f32[1,3,256]{2,0,1:T(1,128)S(1)}, f32[8,3,256]{2,1,0:T(4,128)S(1)}, /...) while((s32[]{:T(128)}, f32[1,32,256]{2,1,0:T(8,128)}, f32[8,32,256]{2,0,1:T(8,128)}, ...), condition=%wide.region_7.8_spmd.clone, body=%wide.region_6.7_spmd.clone.sunk | while | flops 26099716 | bytes 182447 | solution.py:169
  254.4 305.4 %while.34 = (s32[]{:T(128)}, f32[64,32,64]{2,1,0:T(8,128)}, s32[24,64]{1,0:T(8,128)}, f32[128,32,64]{2,1,0:T(8,128)}, f32[64,3,64]{2,0,1:T(8,128)S(1)}, /*index=...) while((s32[]{:T(128)}, f32[64,32,64]{2,1,0:T(8,128)}, s32[24,64]{1,0:T(8,128)}, ...), condition=%wide.region_3.4_spmd.clone, body=%wide.region_2.3_spmd.clone.sunk | while | flops 104596672 | bytes 3020919 | solution.py:116
  271.5 7.5 fusion.221
  284.3 7.5 fusion.221
  297.1 7.5 fusion.221
  309.8 7.5 fusion.221
  399.2 7.5 fusion.221
  424.7 7.5 fusion.221
  437.5 7.5 fusion.221
  450.2 7.5 fusion.221
  475.7 7.5 fusion.221
  488.5 7.5 fusion.221
  501.3 7.5 fusion.221
  514.0 7.5 fusion.221
  566.2 492.9 %while.33 = (s32[]{:T(128)}, f32[64,32,128]{2,1,0:T(8,128)}, s32[27,64]{1,0:T(8,128)}, f32[128,32,128]{2,1,0:T(8,128)}, f32[64,3,128]{2,0,1:T(8,128)S(1)}, /*ind...) while((s32[]{:T(128)}, f32[64,32,128]{2,1,0:T(8,128)}, ...), condition=%wide.region_1.2_spmd.clone, body=%wide.region_0.1_spmd.clone.sunk | while | flops 417858752 | bytes 6035575 | solution.py:116
  572.0 12.5 %fusion.216 = f32[64,32,128]{2,1,0:T(8,128)} fusion(f32[64,32,128]{2,1,0:T(8,128)S(1)} %gather_fusion, f32[64]{0:T(128)S(1)} %dynamic-slice_bitcast_fusion.4, f32[64,128]{1,0:T(8,128)} %bitcast.253, f32[64,128]{1,0:T(8,128)} %get-tuple-element.462, f32[64,128]{1,0:T(8,128)} %bitcast.252, f32[64,128]{1,0:T(8,128)} %get-tuple-element.464, ...), kind=kOutput, calls=%fused_computation.36.clone.1 | convolution fusion | flops 417857536 | bytes 3342593 | tf_op jit(solution)/shard_map/while/body/eval_jaxpr/lab,lvb->lva/dot_general | solution.py:107
  590.0 12.7 %fusion.216 = f32[64,32,128]{2,1,0:T(8,128)} fusion(f32[64,32,128]{2,1,0:T(8,128)S(1)} %gather_fusion, f32[64]{0:T(128)S(1)} %dynamic-slice_bitcast_fusion.4, f32[64,128]{1,0:T(8,128)} %bitcast.253, f32[64,128]{1,0:T(8,128)} %get-tuple-element.462, f32[64,128]{1,0:T(8,128)} %bitcast.252, f32[64,128]{1,0:T(8,128)} %get-tuple-element.464, ...), kind=kOutput, calls=%fused_computation.36.clone.1 | convolution fusion | flops 417857536 | bytes 3342593 | tf_op jit(solution)/shard_map/while/body/eval_jaxpr/lab,lvb->lva/dot_general | solution.py:107
  608.3 12.7 %fusion.216 = f32[64,32,128]{2,1,0:T(8,128)} fusion(f32[64,32,128]{2,1,0:T(8,128)S(1)} %gather_fusion, f32[64]{0:T(128)S(1)} %dynamic-slice_bitcast_fusion.4, f32[64,128]{1,0:T(8,128)} %bitcast.253, f32[64,128]{1,0:T(8,128)} %get-tuple-element.462, f32[64,128]{1,0:T(8,128)} %bitcast.252, f32[64,128]{1,0:T(8,128)} %get-tuple-element.464, ...), kind=kOutput, calls=%fused_computation.36.clone.1 | convolution fusion | flops 417857536 | bytes 3342593 | tf_op jit(solution)/shard_map/while/body/eval_jaxpr/lab,lvb->lva/dot_general | solution.py:107
  626.5 12.7 %fusion.216 = f32[64,32,128]{2,1,0:T(8,128)} fusion(f32[64,32,128]{2,1,0:T(8,128)S(1)} %gather_fusion, f32[64]{0:T(128)S(1)} %dynamic-slice_bitcast_fusion.4, f32[64,128]{1,0:T(8,128)} %bitcast.253, f32[64,128]{1,0:T(8,128)} %get-tuple-element.462, f32[64,128]{1,0:T(8,128)} %bitcast.252, f32[64,128]{1,0:T(8,128)} %get-tuple-element.464, ...), kind=kOutput, calls=%fused_computation.36.clone.1 | convolution fusion | flops 417857536 | bytes 3342593 | tf_op jit(solution)/shard_map/while/body/eval_jaxpr/lab,lvb->lva/dot_general | solution.py:107
  644.8 12.7 %fusion.216 = f32[64,32,128]{2,1,0:T(8,128)} fusion(f32[64,32,128]{2,1,0:T(8,128)S(1)} %gather_fusion, f32[64]{0:T(128)S(1)} %dynamic-slice_bitcast_fusion.4, f32[64,128]{1,0:T(8,128)} %bitcast.253, f32[64,128]{1,0:T(8,128)} %get-tuple-element.462, f32[64,128]{1,0:T(8,128)} %bitcast.252, f32[64,128]{1,0:T(8,128)} %get-tuple-element.464, ...), kind=kOutput, calls=%fused_computation.36.clone.1 | convolution fusion | flops 417857536 | bytes 3342593 | tf_op jit(solution)/shard_map/while/body/eval_jaxpr/lab,lvb->lva/dot_general | solution.py:107
  663.0 12.7 %fusion.216 = f32[64,32,128]{2,1,0:T(8,128)} fusion(f32[64,32,128]{2,1,0:T(8,128)S(1)} %gather_fusion, f32[64]{0:T(128)S(1)} %dynamic-slice_bitcast_fusion.4, f32[64,128]{1,0:T(8,128)} %bitcast.253, f32[64,128]{1,0:T(8,128)} %get-tuple-element.462, f32[64,128]{1,0:T(8,128)} %bitcast.252, f32[64,128]{1,0:T(8,128)} %get-tuple-element.464, ...), kind=kOutput, calls=%fused_computation.36.clone.1 | convolution fusion | flops 417857536 | bytes 3342593 | tf_op jit(solution)/shard_map/while/body/eval_jaxpr/lab,lvb->lva/dot_general | solution.py:107
  681.3 12.7 %fusion.216 = f32[64,32,128]{2,1,0:T(8,128)} fusion(f32[64,32,128]{2,1,0:T(8,128)S(1)} %gather_fusion, f32[64]{0:T(128)S(1)} %dynamic-slice_bitcast_fusion.4, f32[64,128]{1,0:T(8,128)} %bitcast.253, f32[64,128]{1,0:T(8,128)} %get-tuple-element.462, f32[64,128]{1,0:T(8,128)} %bitcast.252, f32[64,128]{1,0:T(8,128)} %get-tuple-element.464, ...), kind=kOutput, calls=%fused_computation.36.clone.1 | convolution fusion | flops 417857536 | bytes 3342593 | tf_op jit(solution)/shard_map/while/body/eval_jaxpr/lab,lvb->lva/dot_general | solution.py:107
  699.6 12.7 %fusion.216 = f32[64,32,128]{2,1,0:T(8,128)} fusion(f32[64,32,128]{2,1,0:T(8,128)S(1)} %gather_fusion, f32[64]{0:T(128)S(1)} %dynamic-slice_bitcast_fusion.4, f32[64,128]{1,0:T(8,128)} %bitcast.253, f32[64,128]{1,0:T(8,128)} %get-tuple-element.462, f32[64,128]{1,0:T(8,128)} %bitcast.252, f32[64,128]{1,0:T(8,128)} %get-tuple-element.464, ...), kind=kOutput, calls=%fused_computation.36.clone.1 | convolution fusion | flops 417857536 | bytes 3342593 | tf_op jit(solution)/shard_map/while/body/eval_jaxpr/lab,lvb->lva/dot_general | solution.py:107
  717.8 12.7 %fusion.216 = f32[64,32,128]{2,1,0:T(8,128)} fusion(f32[64,32,128]{2,1,0:T(8,128)S(1)} %gather_fusion, f32[64]{0:T(128)S(1)} %dynamic-slice_bitcast_fusion.4, f32[64,128]{1,0:T(8,128)} %bitcast.253, f32[64,128]{1,0:T(8,128)} %get-tuple-element.462, f32[64,128]{1,0:T(8,128)} %bitcast.252, f32[64,128]{1,0:T(8,128)} %get-tuple-element.464, ...), kind=kOutput, calls=%fused_computation.36.clone.1 | convolution fusion | flops 417857536 | bytes 3342593 | tf_op jit(solution)/shard_map/while/body/eval_jaxpr/lab,lvb->lva/dot_general | solution.py:107
  736.1 12.7 %fusion.216 = f32[64,32,128]{2,1,0:T(8,128)} fusion(f32[64,32,128]{2,1,0:T(8,128)S(1)} %gather_fusion, f32[64]{0:T(128)S(1)} %dynamic-slice_bitcast_fusion.4, f32[64,128]{1,0:T(8,128)} %bitcast.253, f32[64,128]{1,0:T(8,128)} %get-tuple-element.462, f32[64,128]{1,0:T(8,128)} %bitcast.252, f32[64,128]{1,0:T(8,128)} %get-tuple-element.464, ...), kind=kOutput, calls=%fused_computation.36.clone.1 | convolution fusion | flops 417857536 | bytes 3342593 | tf_op jit(solution)/shard_map/while/body/eval_jaxpr/lab,lvb->lva/dot_general | solution.py:107
  754.3 12.7 %fusion.216 = f32[64,32,128]{2,1,0:T(8,128)} fusion(f32[64,32,128]{2,1,0:T(8,128)S(1)} %gather_fusion, f32[64]{0:T(128)S(1)} %dynamic-slice_bitcast_fusion.4, f32[64,128]{1,0:T(8,128)} %bitcast.253, f32[64,128]{1,0:T(8,128)} %get-tuple-element.462, f32[64,128]{1,0:T(8,128)} %bitcast.252, f32[64,128]{1,0:T(8,128)} %get-tuple-element.464, ...), kind=kOutput, calls=%fused_computation.36.clone.1 | convolution fusion | flops 417857536 | bytes 3342593 | tf_op jit(solution)/shard_map/while/body/eval_jaxpr/lab,lvb->lva/dot_general | solution.py:107
  772.6 12.7 %fusion.216 = f32[64,32,128]{2,1,0:T(8,128)} fusion(f32[64,32,128]{2,1,0:T(8,128)S(1)} %gather_fusion, f32[64]{0:T(128)S(1)} %dynamic-slice_bitcast_fusion.4, f32[64,128]{1,0:T(8,128)} %bitcast.253, f32[64,128]{1,0:T(8,128)} %get-tuple-element.462, f32[64,128]{1,0:T(8,128)} %bitcast.252, f32[64,128]{1,0:T(8,128)} %get-tuple-element.464, ...), kind=kOutput, calls=%fused_computation.36.clone.1 | convolution fusion | flops 417857536 | bytes 3342593 | tf_op jit(solution)/shard_map/while/body/eval_jaxpr/lab,lvb->lva/dot_general | solution.py:107
  790.9 12.7 %fusion.216 = f32[64,32,128]{2,1,0:T(8,128)} fusion(f32[64,32,128]{2,1,0:T(8,128)S(1)} %gather_fusion, f32[64]{0:T(128)S(1)} %dynamic-slice_bitcast_fusion.4, f32[64,128]{1,0:T(8,128)} %bitcast.253, f32[64,128]{1,0:T(8,128)} %get-tuple-element.462, f32[64,128]{1,0:T(8,128)} %bitcast.252, f32[64,128]{1,0:T(8,128)} %get-tuple-element.464, ...), kind=kOutput, calls=%fused_computation.36.clone.1 | convolution fusion | flops 417857536 | bytes 3342593 | tf_op jit(solution)/shard_map/while/body/eval_jaxpr/lab,lvb->lva/dot_general | solution.py:107
  809.1 12.7 %fusion.216 = f32[64,32,128]{2,1,0:T(8,128)} fusion(f32[64,32,128]{2,1,0:T(8,128)S(1)} %gather_fusion, f32[64]{0:T(128)S(1)} %dynamic-slice_bitcast_fusion.4, f32[64,128]{1,0:T(8,128)} %bitcast.253, f32[64,128]{1,0:T(8,128)} %get-tuple-element.462, f32[64,128]{1,0:T(8,128)} %bitcast.252, f32[64,128]{1,0:T(8,128)} %get-tuple-element.464, ...), kind=kOutput, calls=%fused_computation.36.clone.1 | convolution fusion | flops 417857536 | bytes 3342593 | tf_op jit(solution)/shard_map/while/body/eval_jaxpr/lab,lvb->lva/dot_general | solution.py:107
  827.4 12.7 %fusion.216 = f32[64,32,128]{2,1,0:T(8,128)} fusion(f32[64,32,128]{2,1,0:T(8,128)S(1)} %gather_fusion, f32[64]{0:T(128)S(1)} %dynamic-slice_bitcast_fusion.4, f32[64,128]{1,0:T(8,128)} %bitcast.253, f32[64,128]{1,0:T(8,128)} %get-tuple-element.462, f32[64,128]{1,0:T(8,128)} %bitcast.252, f32[64,128]{1,0:T(8,128)} %get-tuple-element.464, ...), kind=kOutput, calls=%fused_computation.36.clone.1 | convolution fusion | flops 417857536 | bytes 3342593 | tf_op jit(solution)/shard_map/while/body/eval_jaxpr/lab,lvb->lva/dot_general | solution.py:107
  845.7 12.7 %fusion.216 = f32[64,32,128]{2,1,0:T(8,128)} fusion(f32[64,32,128]{2,1,0:T(8,128)S(1)} %gather_fusion, f32[64]{0:T(128)S(1)} %dynamic-slice_bitcast_fusion.4, f32[64,128]{1,0:T(8,128)} %bitcast.253, f32[64,128]{1,0:T(8,128)} %get-tuple-element.462, f32[64,128]{1,0:T(8,128)} %bitcast.252, f32[64,128]{1,0:T(8,128)} %get-tuple-element.464, ...), kind=kOutput, calls=%fused_computation.36.clone.1 | convolution fusion | flops 417857536 | bytes 3342593 | tf_op jit(solution)/shard_map/while/body/eval_jaxpr/lab,lvb->lva/dot_general | solution.py:107
  863.9 12.7 %fusion.216 = f32[64,32,128]{2,1,0:T(8,128)} fusion(f32[64,32,128]{2,1,0:T(8,128)S(1)} %gather_fusion, f32[64]{0:T(128)S(1)} %dynamic-slice_bitcast_fusion.4, f32[64,128]{1,0:T(8,128)} %bitcast.253, f32[64,128]{1,0:T(8,128)} %get-tuple-element.462, f32[64,128]{1,0:T(8,128)} %bitcast.252, f32[64,128]{1,0:T(8,128)} %get-tuple-element.464, ...), kind=kOutput, calls=%fused_computation.36.clone.1 | convolution fusion | flops 417857536 | bytes 3342593 | tf_op jit(solution)/shard_map/while/body/eval_jaxpr/lab,lvb->lva/dot_general | solution.py:107
  882.2 12.7 %fusion.216 = f32[64,32,128]{2,1,0:T(8,128)} fusion(f32[64,32,128]{2,1,0:T(8,128)S(1)} %gather_fusion, f32[64]{0:T(128)S(1)} %dynamic-slice_bitcast_fusion.4, f32[64,128]{1,0:T(8,128)} %bitcast.253, f32[64,128]{1,0:T(8,128)} %get-tuple-element.462, f32[64,128]{1,0:T(8,128)} %bitcast.252, f32[64,128]{1,0:T(8,128)} %get-tuple-element.464, ...), kind=kOutput, calls=%fused_computation.36.clone.1 | convolution fusion | flops 417857536 | bytes 3342593 | tf_op jit(solution)/shard_map/while/body/eval_jaxpr/lab,lvb->lva/dot_general | solution.py:107
  900.4 12.7 %fusion.216 = f32[64,32,128]{2,1,0:T(8,128)} fusion(f32[64,32,128]{2,1,0:T(8,128)S(1)} %gather_fusion, f32[64]{0:T(128)S(1)} %dynamic-slice_bitcast_fusion.4, f32[64,128]{1,0:T(8,128)} %bitcast.253, f32[64,128]{1,0:T(8,128)} %get-tuple-element.462, f32[64,128]{1,0:T(8,128)} %bitcast.252, f32[64,128]{1,0:T(8,128)} %get-tuple-element.464, ...), kind=kOutput, calls=%fused_computation.36.clone.1 | convolution fusion | flops 417857536 | bytes 3342593 | tf_op jit(solution)/shard_map/while/body/eval_jaxpr/lab,lvb->lva/dot_general | solution.py:107
  918.7 12.7 %fusion.216 = f32[64,32,128]{2,1,0:T(8,128)} fusion(f32[64,32,128]{2,1,0:T(8,128)S(1)} %gather_fusion, f32[64]{0:T(128)S(1)} %dynamic-slice_bitcast_fusion.4, f32[64,128]{1,0:T(8,128)} %bitcast.253, f32[64,128]{1,0:T(8,128)} %get-tuple-element.462, f32[64,128]{1,0:T(8,128)} %bitcast.252, f32[64,128]{1,0:T(8,128)} %get-tuple-element.464, ...), kind=kOutput, calls=%fused_computation.36.clone.1 | convolution fusion | flops 417857536 | bytes 3342593 | tf_op jit(solution)/shard_map/while/body/eval_jaxpr/lab,lvb->lva/dot_general | solution.py:107
  936.9 12.7 %fusion.216 = f32[64,32,128]{2,1,0:T(8,128)} fusion(f32[64,32,128]{2,1,0:T(8,128)S(1)} %gather_fusion, f32[64]{0:T(128)S(1)} %dynamic-slice_bitcast_fusion.4, f32[64,128]{1,0:T(8,128)} %bitcast.253, f32[64,128]{1,0:T(8,128)} %get-tuple-element.462, f32[64,128]{1,0:T(8,128)} %bitcast.252, f32[64,128]{1,0:T(8,128)} %get-tuple-element.464, ...), kind=kOutput, calls=%fused_computation.36.clone.1 | convolution fusion | flops 417857536 | bytes 3342593 | tf_op jit(solution)/shard_map/while/body/eval_jaxpr/lab,lvb->lva/dot_general | solution.py:107
  955.1 12.7 %fusion.216 = f32[64,32,128]{2,1,0:T(8,128)} fusion(f32[64,32,128]{2,1,0:T(8,128)S(1)} %gather_fusion, f32[64]{0:T(128)S(1)} %dynamic-slice_bitcast_fusion.4, f32[64,128]{1,0:T(8,128)} %bitcast.253, f32[64,128]{1,0:T(8,128)} %get-tuple-element.462, f32[64,128]{1,0:T(8,128)} %bitcast.252, f32[64,128]{1,0:T(8,128)} %get-tuple-element.464, ...), kind=kOutput, calls=%fused_computation.36.clone.1 | convolution fusion | flops 417857536 | bytes 3342593 | tf_op jit(solution)/shard_map/while/body/eval_jaxpr/lab,lvb->lva/dot_general | solution.py:107
  973.4 12.7 %fusion.216 = f32[64,32,128]{2,1,0:T(8,128)} fusion(f32[64,32,128]{2,1,0:T(8,128)S(1)} %gather_fusion, f32[64]{0:T(128)S(1)} %dynamic-slice_bitcast_fusion.4, f32[64,128]{1,0:T(8,128)} %bitcast.253, f32[64,128]{1,0:T(8,128)} %get-tuple-element.462, f32[64,128]{1,0:T(8,128)} %bitcast.252, f32[64,128]{1,0:T(8,128)} %get-tuple-element.464, ...), kind=kOutput, calls=%fused_computation.36.clone.1 | convolution fusion | flops 417857536 | bytes 3342593 | tf_op jit(solution)/shard_map/while/body/eval_jaxpr/lab,lvb->lva/dot_general | solution.py:107
  991.6 12.7 %fusion.216 = f32[64,32,128]{2,1,0:T(8,128)} fusion(f32[64,32,128]{2,1,0:T(8,128)S(1)} %gather_fusion, f32[64]{0:T(128)S(1)} %dynamic-slice_bitcast_fusion.4, f32[64,128]{1,0:T(8,128)} %bitcast.253, f32[64,128]{1,0:T(8,128)} %get-tuple-element.462, f32[64,128]{1,0:T(8,128)} %bitcast.252, f32[64,128]{1,0:T(8,128)} %get-tuple-element.464, ...), kind=kOutput, calls=%fused_computation.36.clone.1 | convolution fusion | flops 417857536 | bytes 3342593 | tf_op jit(solution)/shard_map/while/body/eval_jaxpr/lab,lvb->lva/dot_general | solution.py:107
  1009.9 12.7 %fusion.216 = f32[64,32,128]{2,1,0:T(8,128)} fusion(f32[64,32,128]{2,1,0:T(8,128)S(1)} %gather_fusion, f32[64]{0:T(128)S(1)} %dynamic-slice_bitcast_fusion.4, f32[64,128]{1,0:T(8,128)} %bitcast.253, f32[64,128]{1,0:T(8,128)} %get-tuple-element.462, f32[64,128]{1,0:T(8,128)} %bitcast.252, f32[64,128]{1,0:T(8,128)} %get-tuple-element.464, ...), kind=kOutput, calls=%fused_computation.36.clone.1 | convolution fusion | flops 417857536 | bytes 3342593 | tf_op jit(solution)/shard_map/while/body/eval_jaxpr/lab,lvb->lva/dot_general | solution.py:107
  1028.1 12.7 %fusion.216 = f32[64,32,128]{2,1,0:T(8,128)} fusion(f32[64,32,128]{2,1,0:T(8,128)S(1)} %gather_fusion, f32[64]{0:T(128)S(1)} %dynamic-slice_bitcast_fusion.4, f32[64,128]{1,0:T(8,128)} %bitcast.253, f32[64,128]{1,0:T(8,128)} %get-tuple-element.462, f32[64,128]{1,0:T(8,128)} %bitcast.252, f32[64,128]{1,0:T(8,128)} %get-tuple-element.464, ...), kind=kOutput, calls=%fused_computation.36.clone.1 | convolution fusion | flops 417857536 | bytes 3342593 | tf_op jit(solution)/shard_map/while/body/eval_jaxpr/lab,lvb->lva/dot_general | solution.py:107
  1046.4 12.7 %fusion.216 = f32[64,32,128]{2,1,0:T(8,128)} fusion(f32[64,32,128]{2,1,0:T(8,128)S(1)} %gather_fusion, f32[64]{0:T(128)S(1)} %dynamic-slice_bitcast_fusion.4, f32[64,128]{1,0:T(8,128)} %bitcast.253, f32[64,128]{1,0:T(8,128)} %get-tuple-element.462, f32[64,128]{1,0:T(8,128)} %bitcast.252, f32[64,128]{1,0:T(8,128)} %get-tuple-element.464, ...), kind=kOutput, calls=%fused_computation.36.clone.1 | convolution fusion | flops 417857536 | bytes 3342593 | tf_op jit(solution)/shard_map/while/body/eval_jaxpr/lab,lvb->lva/dot_general | solution.py:107
  1070.3 23.0 %scatter_custom_fusion = f32[32,8192]{0,1:T(8,128)} fusion(s32[8192]{0:T(1024)} %get-tuple-element.323, f32[8192,32]{1,0:T(8,128)} %copy.100, f32[]{:T(128)} %constant.20.clone.1), kind=kCustom, calls=%fused_computation.143 | custom fusion | bytes 1049088 | tf_op jit(solution)/shard_map/scatter | solution.py:192
  (539 shorter events, 528.9 us)
Async XLA Ops:
  0.0 38.6 %copy-start = (f32[64,64,128]{2,1,0:T(8,128)S(1)}, f32[64,64,128]{2,1,0:T(8,128)}, u32[]{:S(2)}) copy-start(f32[64,64,128]{2,1,0:T(8,128)} %param.32) | copy-start | bytes 6291460
  43.2 11.4 %copy-start.6 = (f32[64,3,64]{2,0,1:T(8,128)S(1)}, f32[64,3,64]{2,0,1:T(8,128)}, u32[]{:S(2)}) copy-start(f32[64,3,64]{2,0,1:T(8,128)} %param.28) | copy-start | bytes 147460
  46.2 187.6 %collective-permute-start.3 = (f32[32,2048]{1,0:T(8,128)}, f32[32,2048]{1,0:T(8,128)}, u32[]{:S(2)}, u32[]{:S(2)}) collective-permute-start(f32[32,2048]{1,0:T(8,128)} %slice.136), channel_id=1, source_target_pairs={{1,0},{2,1},{3,2},{4,3},{5,4},{6,5},{7,6},{8,7},{9,8},{10,9},{11,1... | collective-permute-start | bytes 786440 | tf_op jit(solution)/shard_map/ppermute | solution.py:28
  50.1 185.6 %collective-permute-start.2 = (f32[32,2048]{1,0:T(8,128)}, f32[32,2048]{1,0:T(8,128)}, u32[]{:S(2)}, u32[]{:S(2)}) collective-permute-start(f32[32,2048]{1,0:T(8,128)} %slice.134), channel_id=1, source_target_pairs={{0,1},{1,2},{2,3},{3,4},{4,5},{5,6},{6,7},{7,8},{8,9},{9,10},{10,1... | collective-permute-start | bytes 786440 | tf_op jit(solution)/shard_map/ppermute | solution.py:26
  54.7 42.4 %copy-start.8 = (f32[64,3,64]{0,2,1:T(8,128)}, f32[64,3,64]{0,2,1:T(8,128)S(1)}, u32[]{:S(2)}) copy-start(f32[64,3,64]{0,2,1:T(8,128)S(1)} %copy.87) | copy-start | bytes 147460
  105.0 138.6 %collective-permute-start.1 = (f32[32,4672]{1,0:T(8,128)}, f32[32,4672]{1,0:T(8,128)}, u32[]{:S(2)}, u32[]{:S(2)}) collective-permute-start(f32[32,4672]{1,0:T(8,128)} %copy.90), channel_id=1, source_target_pairs={{1,0},{2,1},{3,2},{4,3},{5,4},{6,5},{7,6},{8,7},{9,8},{10,9},{11,1... | collective-permute-start | bytes 1794056 | tf_op jit(solution)/shard_map/ppermute | solution.py:28
  110.1 130.4 %collective-permute-start = (f32[32,4672]{1,0:T(8,128)}, f32[32,4672]{1,0:T(8,128)}, u32[]{:S(2)}, u32[]{:S(2)}) collective-permute-start(f32[32,4672]{1,0:T(8,128)} %copy.89), channel_id=1, source_target_pairs={{0,1},{1,2},{2,3},{3,4},{4,5},{5,6},{6,7},{7,8},{8,9},{9,10},{10,1... | collective-permute-start | bytes 1794056 | tf_op jit(solution)/shard_map/ppermute | solution.py:26
  114.2 3.7 copy-start.5
  114.2 4.4 copy-start.14
  117.9 21.7 %copy-start.25 = (s32[1,4]{1,0:T(1,128)S(1)}, s32[1,4]{1,0:T(1,128)}, u32[]{:S(2)}) copy-start(s32[1,4]{1,0:T(1,128)} %param.27) | copy-start | bytes 52
  117.9 22.9 %copy-start.20 = (s32[8,4]{0,1:T(4,128)S(1)}, s32[8,4]{0,1:T(4,128)}, u32[]{:S(2)}) copy-start(s32[8,4]{0,1:T(4,128)} %param.26) | copy-start | bytes 388
  118.0 31.4 %copy-start.4 = (f32[8,3,128]{2,0,1:T(8,128)S(1)}, f32[8,3,128]{2,0,1:T(8,128)}, u32[]{:S(2)}) copy-start(f32[8,3,128]{2,0,1:T(8,128)} %param.29) | copy-start | bytes 36868
  185.2 34.2 %copy-start.23 = (f32[4,256]{1,0:T(4,128)S(1)}, f32[4,256]{1,0:T(4,128)}, u32[]{:S(2)}) copy-start(f32[4,256]{1,0:T(4,128)} %get-tuple-element.328) | copy-start | bytes 12292
  185.2 34.2 %copy-start.24 = (f32[4,256]{1,0:T(4,128)S(1)}, f32[4,256]{1,0:T(4,128)}, u32[]{:S(2)}) copy-start(f32[4,256]{1,0:T(4,128)} %get-tuple-element.329) | copy-start | bytes 12292
  218.6 3.3 copy-start.17
  218.6 3.3 copy-start.18
  218.6 3.3 copy-start.19
  218.6 3.4 copy-start.21
  218.6 3.4 copy-start.22
  218.6 3.4 copy-start.13
  222.0 4.9 copy-start.15
  222.0 5.5 copy-start.11
  222.0 5.5 copy-start.16
  243.6 3.2 copy-start.9
  246.9 1.7 copy-start.1
  246.9 2.4 copy-start.2
  246.9 3.1 copy-start.3
  250.8 3.6 copy-start.7
  562.8 3.2 copy-start.12
  1060.1 5.3 copy-start.10
where the time goes:
time: 1110 us; the launch traced here: 1100 us
  matrix products  570 us (51%)
  local copies, waits for them, and re-layouts  408 us (37%)
  other arithmetic  54.3 us (5%)
  blocking collectives  50.9 us (5%)
  starting transfers between devices  12 us (1%)
    dot_general x51, matrix products, add_slot(): jnp.einsum('lab,lvb->lva', kernel_tiles, partner_values[slot_ids], precis...  521 us
    gather x51, local copies, waits for them, and re-layouts, add_slot(): partner_values[slot_ids]  112 us
    gather x51, local copies, waits for them, and re-layouts, add_slot(): partner_sets[slot_ids]  56.1 us
    select_n x51, other arithmetic, add_slot(): partner_values[slot_ids]  34.8 us
    mul x51, local copies, waits for them, and re-layouts, add_slot(): matern(anchor_sets, partner_sets[slot_ids]) * slot_mask[:, None, None]  34.7 us
    gather x1, local copies, waits for them, and re-layouts, body(): probes[:, morton].reshape(probe_count, leaf_count, P_SIZE)  29.9 us
    gather x1, local copies, waits for them, and re-layouts, body(): points[:, morton].reshape(3, leaf_count, P_SIZE).transpose(1, 0, 2)  29.9 us
    scatter x2, local copies, waits for them, and re-layouts, body(): return jnp.zeros_like(ordered).at[:, morton].set(ordered)  26.6 us
  transfers between devices with their start and end apart: 4, of which 0 were waited for; matrix products, arithmetic and copies ran while one was open for 12% of the time, Pallas kernels for 0%

commit v1 on v0

v1 whole, which is shorter than its diff:
```python
import functools
import math

import jax
import jax.numpy as jnp
from jax import lax
from jax.experimental import pallas as pl
from jax.experimental.pallas import tpu as pltpu
from jax.sharding import PartitionSpec as P

P_SIZE = 128
CH = 8
HALO = 32
NEAR_STEP = 3
FAR_STEP = 2

highest = lax.Precision.HIGHEST
scale = math.sqrt(3.0) / 12.0 * math.log2(math.e)
soft = 0.0001 * scale * scale
ln2 = math.log(2.0)
f32 = jnp.float32
bf16 = jnp.bfloat16
NT = (((1,), (1,)), ((), ()))


def hdot(a, b):
    return jnp.dot(a, b, precision=highest, preferred_element_type=f32)


def hdot_nt(a, b):
    return lax.dot_general(a, b, NT, precision=highest, preferred_element_type=f32)


def profile(squared):
    squared = jnp.maximum(squared, soft)
    u = squared * lax.rsqrt(squared)
    return (1.0 + ln2 * u) * jnp.exp2(-u)


def split3(v):
    high = v.astype(bf16).astype(f32)
    rest = v - high
    mid = rest.astype(bf16).astype(f32)
    return high, mid, rest - mid


def augmented(x):
    row = lax.broadcasted_iota(jnp.int32, x.shape, 0)
    norm = jnp.sum(x * x, axis=0, keepdims=True)
    source = jnp.where(row < 3, -2.0 * x, jnp.where(row == 3, 1.0, jnp.where(row == 4, norm + soft, 0.0)))
    target = jnp.where(row < 3, x, jnp.where(row == 3, norm, jnp.where(row == 4, 1.0, 0.0)))
    return source, target


def source_rows(v):
    h, m, lo = split3(v)
    return jnp.concatenate([h, m, h, m, lo, h, lo, m], axis=0)


def target_rows(v):
    h, m, lo = split3(v)
    return jnp.concatenate([h, h, m, m, h, lo, m, lo], axis=0)


def coords(block, centre):
    row = lax.broadcasted_iota(jnp.int32, block.shape, 0)
    return jnp.where(row < 3, (block - centre) * scale, 0.0)


def arrange_kernel(
    morton, points, probes, skel, basis, leaf_tr, box_tr, sub_tr,
    geo, q1_out, q2_out, q3_out, rows, pad, got,
):
    leaves = geo.shape[0]
    boxes = q1_out.shape[0]
    pad[...] = jnp.zeros_like(pad)

    def flip(i, c):
        at = pl.ds(pl.multiple_of(i * P_SIZE, P_SIZE), P_SIZE)
        pad[0:32, :] = probes[:, at]
        pad[32:35, :] = points[:, at]
        rows[at, :] = pad[...].T
        return c

    lax.fori_loop(0, leaves, flip, 0)

    def one_leaf(i, j, acc):
        base = i * P_SIZE
        for k in range(P_SIZE):
            got[j, k : k + 1, :] = rows[pl.ds(morton[base + k], 1), :]
        turned = got[j].T
        geo[i, 0:40, :] = turned[0:40]
        geo[i, 35:38, 0:64] = skel[i]
        q0 = hdot_nt(turned[0:32], basis[i])
        geo[i, 40:56, 0:64] = q0[0:16]
        geo[i, 40:56, 64:128] = q0[16:32]
        return acc + hdot(q0, leaf_tr[i])

    def one_box(b, q2):
        def pair(h, acc):
            for j in range(2):
                acc = one_leaf(b * CH + h * 2 + j, j, acc)
            return acc

        q1 = lax.fori_loop(0, CH // 2, pair, jnp.zeros(q1_out.shape[1:], f32))
        q1_out[b] = q1
        return q2 + hdot(q1, box_tr[b])

    q2 = lax.fori_loop(0, boxes, one_box, jnp.zeros(q2_out.shape, f32))
    q2_out[...] = q2
    q3_out[...] = hdot(q2, sub_tr[0])


def couple_kernel(
    near_ids, near_trips, far_ids, far_trips, left, own, right,
    near_out, far_out, src, tgt, xw, src_lo, src_hi, tgt2, qw,
    *, near_width, far_width, near_factor, far_factor,
):
    leaves = own.shape[0]
    total = leaves + 2 * HALO
    first = own[0, 32:40, 0:1]
    centre_pt = first
    centre_sk = jnp.concatenate([first[3:8], first[0:3]], axis=0)

    def prepare(ref, i, at, local):
        block = ref[i, 32:40, :]
        s8, t8 = augmented(coords(block, centre_pt))
        src[at] = source_rows(s8).T.astype(bf16)
        lane = lax.broadcasted_iota(jnp.int32, (8, P_SIZE), 1)
        turned = jnp.concatenate([block[3:8], block[0:3]], axis=0)
        ks8, kt8 = augmented(coords(turned, centre_sk))
        both = source_rows(ks8)
        zero = jnp.zeros_like(both)
        src_lo[at] = jnp.concatenate([both, zero], axis=0).T[0:64].astype(bf16)
        src_hi[at] = jnp.concatenate([zero, both], axis=0).T[0:64].astype(bf16)
        x = ref[i, 0:32, :]
        hi = x.astype(bf16)
        lo = (x - hi.astype(f32)).astype(bf16)
        xw[at, :, 0:128] = jnp.concatenate([hi, lo], axis=0)
        xw[at, :, 128:256] = jnp.concatenate([hi, jnp.zeros_like(lo)], axis=0)
        q = ref[i, 40:56, :]
        qr = pltpu.roll(q, 64, 1)
        low = lax.broadcasted_iota(jnp.int32, (16, P_SIZE), 1) < 64
        twice = jnp.concatenate([jnp.where(low, q, qr), jnp.where(low, qr, q)], axis=0)
        qhi = twice.astype(bf16)
        low2 = lax.broadcasted_iota(jnp.int32, (32, P_SIZE), 1) < 64
        qlo = jnp.where(low2, twice - qhi.astype(f32), 0.0).astype(bf16)
        qw[at] = jnp.concatenate([qhi, qlo], axis=0)
        if local is not None:
            tgt[i] = target_rows(t8).astype(bf16)
            kt8 = jnp.where(lane < 64, kt8, 0.0)
            if local == 1:
                kt8 = pltpu.roll(kt8, 64, 1)
            return target_rows(kt8).astype(bf16)
        return None

    def halo(i, c):
        prepare(left, i, i, None)
        prepare(right, i, i + HALO + leaves, None)
        return c

    lax.fori_loop(0, HALO, halo, 0)

    def middle(p, c):
        for j in range(2):
            i = p * 2 + j
            tgt2[p, j * 64 : j * 64 + 64, :] = prepare(own, i, i + HALO, j)
        return c

    lax.fori_loop(0, leaves // 2, middle, 0)
    src[total] = jnp.zeros(src.shape[1:], bf16)
    xw[total] = jnp.zeros(xw.shape[1:], bf16)
    src_lo[total] = jnp.zeros(src_lo.shape[1:], bf16)
    src_hi[total] = jnp.zeros(src_hi.shape[1:], bf16)
    qw[total] = jnp.zeros(qw.shape[1:], bf16)

    def near_leaf(l, c):
        target = tgt[l]

        def step(t, acc):
            tiles, values = [], []
            for u in range(NEAR_STEP):
                m = near_ids[l * near_width + t * NEAR_STEP + u]
                k = profile(jnp.dot(src[m], target, preferred_element_type=f32))
                hi = k.astype(bf16)
                tiles += [hi, (k - hi.astype(f32)).astype(bf16)]
                values.append(xw[m])
            return acc + jnp.dot(
                jnp.concatenate(values, axis=1),
                jnp.concatenate(tiles, axis=0),
                preferred_element_type=f32,
            )

        acc = lax.fori_loop(0, near_trips[l], step, jnp.zeros((64, P_SIZE), f32))
        near_out[l] = (acc[0:32] + acc[32:64]) * near_factor
        return c

    lax.fori_loop(0, leaves, near_leaf, 0)

    def far_pair(p, c):
        target = tgt2[p]

        def step(t, acc):
            tiles, values = [], []
            for u in range(FAR_STEP):
                at = t * FAR_STEP + u
                a = far_ids[2 * p * far_width + at]
                b = far_ids[(2 * p + 1) * far_width + at]
                k = profile(
                    jnp.dot(src_lo[a] + src_hi[b], target, preferred_element_type=f32)
                )
                hi = k.astype(bf16)
                tiles += [hi, (k - hi.astype(f32)).astype(bf16)]
                values.append(jnp.concatenate([qw[a], qw[b]], axis=0))
            return acc + jnp.dot(
                jnp.concatenate(values, axis=1),
                jnp.concatenate(tiles, axis=0),
                preferred_element_type=f32,
            )

        acc = lax.fori_loop(0, far_trips[p], step, jnp.zeros((128, P_SIZE), f32))
        low = lax.broadcasted_iota(jnp.int32, (32, P_SIZE), 1) < 64
        far_out[p] = (
            jnp.where(low, acc[0:32] + acc[32:64], acc[64:96] + acc[96:128]) * far_factor
        )
        return c

    lax.fori_loop(0, leaves // 2, far_pair, 0)


def centred(block, centre):
    return augmented(coords(block, centre))


def finish_kernel(
    morton, box_far, sub_far, place,
    near, far, q1, gathered, box_skel, group_skel,
    basis, leaf_tr, box_tr, sub_tr,
    out, rows, pad, l1s,
    *, subs, groups, box_width, sub_width, f1, f2, f3,
):
    boxes = q1.shape[0]
    leaves = near.shape[0]
    device, group = place[0], place[1]

    def tile(source8, target8):
        return profile(
            jnp.dot(
                source_rows(source8).T.astype(bf16),
                target_rows(target8).astype(bf16),
                preferred_element_type=f32,
            )
        )

    own = gathered[device, 64:72, :]
    centre = own[:, 0:1]
    target = centred(own, centre)[1]

    def sub_term(j, acc):
        entry = sub_far[j]
        m = jnp.maximum(entry, 0)
        source = centred(gathered[m, 64:72, :], centre)[0]
        term = hdot(gathered[m, 0:32, :], tile(source, target))
        return acc + jnp.where(entry >= 0, term, 0.0)

    z2 = lax.fori_loop(0, sub_width, sub_term, jnp.zeros(gathered[0, 0:32, :].shape, f32))
    g_own = group_skel[group]
    g_centre = g_own[:, 0:1]
    g_target = centred(g_own, g_centre)[1]

    def group_term(h, acc):
        q3 = lax.fori_loop(
            0, subs, lambda s, t: t + gathered[h * subs + s, 32:64, :], jnp.zeros(z2.shape, f32)
        )
        source = centred(group_skel[h], g_centre)[0]
        return acc + jnp.where(h != group, hdot(q3, tile(source, g_target)), 0.0)

    z3 = lax.fori_loop(0, groups, group_term, jnp.zeros(z2.shape, f32))
    l2 = z2 * f2 + hdot_nt(z3 * f3, sub_tr[0])

    def box_level(b, c):
        mine = box_skel[b]
        b_centre = mine[:, 0:1]
        b_target = centred(mine, b_centre)[1]

        def box_term(j, acc):
            entry = box_far[b * box_width + j]
            m = jnp.maximum(entry - device * boxes, 0)
            source = centred(box_skel[m], b_centre)[0]
            return acc + jnp.where(entry >= 0, hdot(q1[m], tile(source, b_target)), 0.0)

        z1 = lax.fori_loop(0, box_width, box_term, jnp.zeros((32, P_SIZE), f32))
        l1s[b] = z1 * f1 + hdot_nt(l2, box_tr[b])
        return c

    lax.fori_loop(0, boxes, box_level, 0)

    pad[...] = jnp.zeros_like(pad)

    def down(p, c):
        l1 = l1s[p // (CH // 2)]
        z = far[p]
        for j in range(2):
            i = 2 * p + j
            l0 = z[:, 64 * j : 64 * j + 64] + hdot_nt(l1, leaf_tr[i])
            y = near[i] + hdot(l0, basis[i])
            pad[j, 0:32, :] = y
            turned = pad[j].T
            pad[2 + j] = turned
            base = i * P_SIZE
            for k in range(P_SIZE):
                rows[pl.ds(morton[base + k], 1), :] = pad[2 + j, k : k + 1, :]
        return c

    lax.fori_loop(0, leaves // 2, down, 0)

    def flip(i, c):
        at = pl.ds(pl.multiple_of(i * P_SIZE, P_SIZE), P_SIZE)
        out[:, at] = rows[at, :].T[0:32]
        return c

    lax.fori_loop(0, leaves, flip, 0)


VMEM = pl.BlockSpec(memory_space=pltpu.VMEM)
SMEM = pl.BlockSpec(memory_space=pltpu.SMEM)
params = pltpu.CompilerParams(vmem_limit_bytes=56 * 2**20)


def slots(ids, base, total, step):
    width = ids.shape[1]
    usable = ids >= 0
    local = jnp.where(usable, ids - base, total)
    more = -width % step
    local = jnp.pad(local, ((0, 0), (0, more)), constant_values=total)
    last = jnp.max(jnp.where(usable, jnp.arange(1, width + 1, dtype=jnp.int32)[None], 0), axis=1)
    return local.reshape(-1), (last + step - 1) // step, width + more


def body(
    points, probes, morton, near_list, leaf_far, box_far, subtree_far,
    leaf_skeleton, box_skeleton, subtree_skeleton, group_skeleton,
    leaf_basis, leaf_transfer, box_transfer, subtree_transfer,
):
    leaves = near_list.shape[0]
    count = points.shape[1]
    nv = probes.shape[0]
    boxes = box_far.shape[0]
    r0, r1 = leaf_basis.shape[1], box_transfer.shape[1]
    r2, r3 = subtree_transfer.shape[1:]
    device = lax.axis_index(("group", "sub"))
    group = lax.axis_index("group")
    subs, groups = lax.axis_size("sub"), lax.axis_size("group")
    total = leaves + 2 * HALO

    geo, q1, q2, q3 = pl.pallas_call(
        arrange_kernel,
        out_shape=(
            jax.ShapeDtypeStruct((leaves, 56, P_SIZE), f32),
            jax.ShapeDtypeStruct((boxes, nv, r1), f32),
            jax.ShapeDtypeStruct((nv, r2), f32),
            jax.ShapeDtypeStruct((nv, r3), f32),
        ),
        in_specs=[SMEM] + [VMEM] * 7,
        out_specs=(VMEM,) * 4,
        scratch_shapes=[
            pltpu.VMEM((count, P_SIZE), f32),
            pltpu.VMEM((P_SIZE, P_SIZE), f32),
            pltpu.VMEM((2, P_SIZE, P_SIZE), f32),
        ],
        compiler_params=params,
        name="arrange",
    )(morton, points, probes, leaf_skeleton, leaf_basis, leaf_transfer, box_transfer, subtree_transfer)

    both = ("group", "sub")
    ends = subs * groups - 1
    left = lax.ppermute(geo[leaves - HALO :], both, [(i, i + 1) for i in range(ends)])
    right = lax.ppermute(geo[:HALO], both, [(i + 1, i) for i in range(ends)])
    packed = jnp.concatenate(
        [q2, q3, subtree_skeleton[0], jnp.zeros((5, r2), f32)], axis=0
    )
    gathered = lax.all_gather(packed, both, axis=0)

    base = device * leaves - HALO
    near_ids, near_trips, near_width = slots(near_list, base, total, NEAR_STEP)
    far_ids, far_trips, far_width = slots(leaf_far, base, total, FAR_STEP)
    far_trips = jnp.max(far_trips.reshape(-1, 2), axis=1)
    near, far = pl.pallas_call(
        functools.partial(
            couple_kernel,
            near_width=near_width,
            far_width=far_width,
            near_factor=(P_SIZE * near_list.shape[1]) ** -0.5,
            far_factor=(r0 * leaf_far.shape[1]) ** -0.5,
        ),
        out_shape=(
            jax.ShapeDtypeStruct((leaves, nv, P_SIZE), f32),
            jax.ShapeDtypeStruct((leaves // 2, nv, P_SIZE), f32),
        ),
        in_specs=[SMEM] * 4 + [VMEM] * 3,
        out_specs=(VMEM,) * 2,
        scratch_shapes=[
            pltpu.VMEM((total + 1, P_SIZE, 64), bf16),
            pltpu.VMEM((leaves, 64, P_SIZE), bf16),
            pltpu.VMEM((total + 1, 64, 256), bf16),
            pltpu.VMEM((total + 1, 64, P_SIZE), bf16),
            pltpu.VMEM((total + 1, 64, P_SIZE), bf16),
            pltpu.VMEM((leaves // 2, P_SIZE, P_SIZE), bf16),
            pltpu.VMEM((total + 1, 64, P_SIZE), bf16),
        ],
        compiler_params=params,
        cost_estimate=pl.CostEstimate(flops=2 * 10**10, bytes_accessed=10**7, transcendentals=5 * 10**7),
        name="couple",
    )(near_ids, near_trips, far_ids, far_trips, left, geo, right)

    pad8 = lambda a: jnp.pad(a, ((0, 0), (0, 5), (0, 0)))
    return pl.pallas_call(
        functools.partial(
            finish_kernel,
            subs=subs,
            groups=groups,
            box_width=box_far.shape[1],
            sub_width=subtree_far.shape[1],
            f1=(r1 * box_far.shape[1]) ** -0.5,
            f2=(r2 * subtree_far.shape[1]) ** -0.5,
            f3=r3**-0.5,
        ),
        out_shape=jax.ShapeDtypeStruct((nv, count), f32),
        in_specs=[SMEM] * 4 + [VMEM] * 10,
        out_specs=VMEM,
        scratch_shapes=[
            pltpu.VMEM((count, P_SIZE), f32),
            pltpu.VMEM((4, P_SIZE, P_SIZE), f32),
            pltpu.VMEM((boxes, nv, P_SIZE), f32),
        ],
        compiler_params=params,
        name="finish",
    )(
        morton, box_far.reshape(-1), subtree_far.reshape(-1),
        jnp.stack([device, group]).astype(jnp.int32),
        near, far, q1, gathered, pad8(box_skeleton), pad8(group_skeleton),
        leaf_basis, leaf_transfer, box_transfer, subtree_transfer,
    )


def solution(mesh):
    two = ("group", "sub")
    placed = (
        (P(None, two),) * 2
        + (P(two),)
        + (P(two, None),) * 4
        + (P(two, None, None),) * 3
        + (P(),)
        + (P(two, None, None),) * 4
    )
    return jax.shard_map(
        body, mesh=mesh, in_specs=placed, out_specs=P(None, two), check_vma=False
    )
```

time: 1110 us -> 427 us (0.38)
  matrix products: 570 us -> 0 us
  local copies, waits for them, and re-layouts: 408 us -> 7.67 us
  Pallas kernels: 0 us -> 372 us
  blocking collectives: 50.9 us -> 0 us
  other arithmetic: 54.3 us -> 3.64 us
  waiting for transfers between devices: 0.01 us -> 18.6 us
  between operations: 0.39 us -> 13.5 us
    dot_general x69 -> x0, matrix products: 570 us -> none  [the longest x51 521 us: add_slot(): jnp.einsum('lab,lvb->lva', kernel_tiles, partner_values[slot_ids], precis...]
    pallas_call x0 -> x3, Pallas kernels: none -> 372 us  [the longest x1 274 us: body(): pl.pallas_call(functools.partial(couple_kernel, near_width=near_width, fa...]
    gather x106 -> x0, local copies, waits for them, and re-layouts: 230 us -> none  [the longest x51 112 us: add_slot(): partner_values[slot_ids]]
    slice x77 -> x1, local copies, waits for them, and re-layouts: 38.8 us -> 1.58 us  [body(): right = lax.ppermute(geo[:HALO], both, [(i + 1, i) for i in range(ends)])]
    select_n x52 -> x1, other arithmetic: 35.4 us -> 0.6 us  [slots(): return (local.reshape(-1), (last + step - 1) // step, width + more)]
    mul x51 -> x0, local copies, waits for them, and re-layouts: 34.7 us -> none  [add_slot(): matern(anchor_sets, partner_sets[slot_ids]) * slot_mask[:, None, None]]
    all_gather x2 -> x0, blocking collectives: 28.4 us -> none  [the longest x1 20.2 us: body(): segment = lax.all_gather(packed_subtree, 'sub', axis=0, tiled=True)]
    scatter x2 -> x0, local copies, waits for them, and re-layouts: 26.6 us -> none  [body(): return jnp.zeros_like(ordered).at[:, morton].set(ordered)]
  transfers between devices with their start and end apart: 4 -> 3, of which waited for: 0 -> 2; matrix products, arithmetic and copies ran while one was open for 12% -> 2% of each run, Pallas kernels for 0% -> 65%
where the time goes in v1:
time: 427 us; the launch traced here: 422 us
  Pallas kernels  372 us (87%)
  waiting for transfers between devices  18.6 us (4%)
  between operations  13.5 us (3%)
  local copies, waits for them, and re-layouts  7.67 us (2%)
  starting transfers between devices  6.51 us (2%)
    pallas_call x1, Pallas kernels, body(): pl.pallas_call(functools.partial(couple_kernel, near_width=near_width, fa...  274 us
    pallas_call x1, Pallas kernels, body(): pl.pallas_call(functools.partial(finish_kernel, subs=subs, groups=groups,...  60.8 us
    pallas_call x1, Pallas kernels, body(): pl.pallas_call(arrange_kernel, out_shape=(jax.ShapeDtypeStruct((leaves, 5...  36.8 us
    ppermute x1, waiting for transfers between devices, body(): right = lax.ppermute(geo[:HALO], both, [(i + 1, i) for i in range(ends)])  15.2 us
  transfers between devices with their start and end apart: 3, of which 2 were waited for; matrix products, arithmetic and copies ran while one was open for 2% of the time, Pallas kernels for 65%

profile of v1, /device:TPU:1, one launch (start us, length us, event | category | flops | bytes accessed | tf_op | source)
XLA Modules:
  0.0 421.7 jit_solution(228515768732947483)
XLA Ops:
  6.5 0.0 all-gather.3.cloned.1.call-start
  6.5 1.6 copy.23.skel
  8.2 0.7 copy.28
  8.8 0.1 pad.13.clone
  8.9 36.8 %arrange.1 = (f32[64,56,128]{2,1,0:T(8,128)}, f32[8,32,128]{2,1,0:T(8,128)}, f32[32,256]{1,0:T(8,128)}, f32[32,256]{1,0:T(8,128)}) custom-call(s32[8192]{0:T(1024)} %morton.3, f32[3,8192]{1,0:T(4,128)} %points.1, f32[32,8192]{1,0:T(8,128)} %probes.1, f32[64,3,64]{2,1,0:T(4,128)} %copy.23.skel, f32[64,64,128]{2,1,0:T(8,128)} %basis.3, ...), custom_call_target="tpu_custom_call" | custom-call | tf_op jit(solution)/shard_map/arrange/pallas_call | solution.py:356
  45.7 0.0 copy-start
  45.8 0.0 copy-start.3
  45.8 0.0 copy-start.1
  45.8 0.0 copy-start.2
  45.8 1.5 maximum_maximum_fusion
  47.3 0.0 copy-start.4
  47.3 0.0 all-gather.3.cloned.1.call-update
  47.3 1.6 fusion.3
  48.9 4.6 %collective-permute-start = (f32[32,56,128]{2,1,0:T(8,128)S(1)}, f32[32,56,128]{2,1,0:T(8,128)S(1)}, u32[]{:S(2)}, u32[]{:S(2)}) collective-permute-start(f32[32,56,128]{2,1,0:T(8,128)S(1)} %get-tuple-element.18), channel_id=1, source_target_pairs={{0,1},{1,2},{2,3},{3,4},{4,5},{5,6},{6,7},{7,8},{8,9},{9,10},{10,1... | collective-permute-start | bytes 2752520 | tf_op jit(solution)/shard_map/ppermute | solution.py:377
  53.5 1.9 collective-permute-start.1
  55.5 0.0 copy-done
  55.5 0.1 select_reduce_fusion
  55.6 0.1 copy.21
  55.7 0.7 reshape.26.near_ids
  56.4 0.0 copy-done.3
  56.4 0.1 select_reduce_fusion.1
  56.5 0.1 copy.22
  56.6 0.7 reshape.27.far_ids
  57.2 0.1 sub.46
  57.3 0.0 copy-done.1
  57.4 0.6 pad.8.box_skel
  58.0 0.0 copy-done.2
  58.0 0.6 pad.9.group_skel
  58.6 0.0 copy-done.4
  58.6 0.1 copy.20
  58.7 0.7 reshape.24.box_far
  59.4 0.7 pad_add_fusion.place
  60.0 0.7 fusion.1.far_trips
  60.7 0.6 and_select_fusion.near_trips
  61.3 3.4 collective-permute-done.left
  64.7 0.0 copy-start.5
  64.7 15.2 %collective-permute-done.1.right = f32[32,56,128]{2,1,0:T(8,128)} collective-permute-done((f32[32,56,128]{2,1,0:T(8,128)S(1)}, f32[32,56,128]{2,1,0:T(8,128)}, u32[]{:S(2)}, u32[]{:S(2)}) %collective-permute-start.1) | collective-permute-done | bytes 917536 | tf_op jit(solution)/shard_map/ppermute | solution.py:378
  79.9 0.0 copy-done.5
  79.9 274.2 %couple.1 = (f32[64,32,128]{2,1,0:T(8,128)}, f32[32,32,128]{2,1,0:T(8,128)}) custom-call(s32[1728]{0:T(1024)} %reshape.26.near_ids, s32[64]{0:T(128)} %and_select_fusion.near_trips, s32[1536]{0:T(1024)} %reshape.27.far_ids, s32[32]{0:T(128)} %fusion.1.far_trips, f32[32,56,128]{2,1,0:T(8,128)} %copy-done.5, f32[64,56,128]{2,1,0:T(8,128)} %get-tuple-element.11.own, ...), custom_call_target="tpu_custom_call" | custom-call | flops 20000000000 | bytes 10000000 | tf_op jit(solution)/shard_map/couple/pallas_call | solution.py:388
  354.1 0.0 all-gather.3.cloned.1.call-done
  354.1 60.8 %finish.1 = f32[32,8192]{1,0:T(8,128)} custom-call(s32[8192]{0:T(1024)} %morton.3, s32[32]{0:T(128)} %reshape.24.box_far, s32[4]{0:T(128)} %bitcast.9, s32[2]{0:T(128)} %pad_add_fusion.place, f32[64,32,128]{2,1,0:T(8,128)} %get-tuple-element.12.near, f32[32,32,128]{2,1,0:T(8,128)} %get-tuple-element.13.far, f32[8,32,128]{2,1,0:T(8,128)} %get-tuple-element.14.q1, ...), custom_call_target="tpu_custom_call" | custom-call | tf_op jit(solution)/shard_map/finish/pallas_call | solution.py:417
  (6 shorter events, 0.0 us)
Async XLA Ops:
  6.5 347.5 %all-gather.3.cloned.1.call-start = ((), (), s32[]{:S(2)}) async-start(), calls=%async_computation | async-start | bytes 2433024 | tf_op jit(solution)/shard_map/all_gather | solution.py:382
  45.7 9.7 %copy-start = (s32[64,27]{0,1:T(8,128)S(1)}, s32[64,27]{0,1:T(8,128)}, u32[]{:S(2)}) copy-start(s32[64,27]{0,1:T(8,128)} %param.18) | copy-start | bytes 20740
  45.8 10.6 %copy-start.3 = (s32[64,24]{0,1:T(8,128)S(1)}, s32[64,24]{0,1:T(8,128)}, u32[]{:S(2)}) copy-start(s32[64,24]{0,1:T(8,128)} %param.19) | copy-start | bytes 18436
  45.8 11.6 %copy-start.1 = (f32[8,3,128]{2,0,1:T(8,128)S(1)}, f32[8,3,128]{2,0,1:T(8,128)}, u32[]{:S(2)}) copy-start(f32[8,3,128]{2,0,1:T(8,128)} %param.23) | copy-start | bytes 36868
  45.8 12.2 %copy-start.2 = (f32[4,3,256]{2,0,1:T(4,128)S(1)}, f32[4,3,256]{2,0,1:T(4,128)}, u32[]{:S(2)}) copy-start(f32[4,3,256]{2,0,1:T(4,128)} %param.25) | copy-start | bytes 36868
  47.3 11.3 %copy-start.4 = (s32[8,4]{0,1:T(4,128)S(1)}, s32[8,4]{0,1:T(4,128)}, u32[]{:S(2)}) copy-start(s32[8,4]{0,1:T(4,128)} %param.20) | copy-start | bytes 388
  48.9 15.8 %collective-permute-start = (f32[32,56,128]{2,1,0:T(8,128)S(1)}, f32[32,56,128]{2,1,0:T(8,128)S(1)}, u32[]{:S(2)}, u32[]{:S(2)}) collective-permute-start(f32[32,56,128]{2,1,0:T(8,128)S(1)} %get-tuple-element.18), channel_id=1, source_target_pairs={{0,1},{1,2},{2,3},{3,4},{4,5},{5,6},{6,7},{7,8},{8,9},{9,10},{10,1... | collective-permute-start | bytes 2752520 | tf_op jit(solution)/shard_map/ppermute | solution.py:377
  53.5 26.4 %collective-permute-start.1 = (f32[32,56,128]{2,1,0:T(8,128)S(1)}, f32[32,56,128]{2,1,0:T(8,128)}, u32[]{:S(2)}, u32[]{:S(2)}) collective-permute-start(f32[32,56,128]{2,1,0:T(8,128)S(1)} %get-tuple-element.17), channel_id=1, source_target_pairs={{1,0},{2,1},{3,2},{4,3},{5,4},{6,5},{7,6},{8,7},{9,8},{10,9},{11,1... | collective-permute-start | bytes 2752520 | tf_op jit(solution)/shard_map/ppermute | solution.py:378
  64.7 15.2 %copy-start.5 = (f32[32,56,128]{2,1,0:T(8,128)}, f32[32,56,128]{2,1,0:T(8,128)S(1)}, u32[]{:S(2)}) copy-start(f32[32,56,128]{2,1,0:T(8,128)S(1)} %collective-permute-done.left) | copy-start | bytes 2752516
Sparse Core Ops, SparseCore 0:
  47.4 60.8 all-gather.2

commit v2 on v1

--- a/solution.py
+++ b/solution.py
@@ -12,7 +12,7 @@
 CH = 8
 HALO = 32
 NEAR_STEP = 3
-FAR_STEP = 2
+FAR_STEP = 4
 
 highest = lax.Precision.HIGHEST
 scale = math.sqrt(3.0) / 12.0 * math.log2(math.e)
@@ -75,34 +75,37 @@
     boxes = q1_out.shape[0]
     pad[...] = jnp.zeros_like(pad)
 
-    def flip(i, c):
-        at = pl.ds(pl.multiple_of(i * P_SIZE, P_SIZE), P_SIZE)
-        pad[0:32, :] = probes[:, at]
-        pad[32:35, :] = points[:, at]
-        rows[at, :] = pad[...].T
-        return c
-
-    lax.fori_loop(0, leaves, flip, 0)
-
-    def one_leaf(i, j, acc):
-        base = i * P_SIZE
-        for k in range(P_SIZE):
-            got[j, k : k + 1, :] = rows[pl.ds(morton[base + k], 1), :]
-        turned = got[j].T
-        geo[i, 0:40, :] = turned[0:40]
-        geo[i, 35:38, 0:64] = skel[i]
-        q0 = hdot_nt(turned[0:32], basis[i])
-        geo[i, 40:56, 0:64] = q0[0:16]
-        geo[i, 40:56, 64:128] = q0[16:32]
-        return acc + hdot(q0, leaf_tr[i])
+    def flip(g, c):
+        for j in range(4):
+            at = pl.ds(pl.multiple_of((4 * g + j) * P_SIZE, P_SIZE), P_SIZE)
+            pad[j, 0:32, :] = probes[:, at]
+            pad[j, 32:35, :] = points[:, at]
+        for j in range(4):
+            at = pl.ds(pl.multiple_of((4 * g + j) * P_SIZE, P_SIZE), P_SIZE)
+            rows[at, :] = pad[j].T
+        return c
+
+    lax.fori_loop(0, leaves // 4, flip, 0)
 
     def one_box(b, q2):
-        def pair(h, acc):
-            for j in range(2):
-                acc = one_leaf(b * CH + h * 2 + j, j, acc)
-            return acc
-
-        q1 = lax.fori_loop(0, CH // 2, pair, jnp.zeros(q1_out.shape[1:], f32))
+        for j in range(CH):
+            base = (b * CH + j) * P_SIZE
+            for k in range(P_SIZE):
+                got[j, k : k + 1, :] = rows[pl.ds(morton[base + k], 1), :]
+        turned = [got[j].T for j in range(CH)]
+        parts = []
+        for j in range(CH):
+            i = b * CH + j
+            geo[i, 0:40, :] = turned[j][0:40]
+            geo[i, 35:38, 0:64] = skel[i]
+            q0 = hdot_nt(turned[j][0:32], basis[i])
+            geo[i, 40:56, 0:64] = q0[0:16]
+            geo[i, 40:56, 64:128] = q0[16:32]
+            parts.append(q0)
+        q1 = jnp.zeros(q1_out.shape[1:], f32)
+        for j in range(0, CH, 2):
+            two = jnp.concatenate([leaf_tr[b * CH + j], leaf_tr[b * CH + j + 1]], axis=0)
+            q1 = q1 + hdot(jnp.concatenate(parts[j : j + 2], axis=1), two)
         q1_out[b] = q1
         return q2 + hdot(q1, box_tr[b])
 
@@ -154,20 +157,25 @@
             return target_rows(kt8).astype(bf16)
         return None
 
-    def halo(i, c):
-        prepare(left, i, i, None)
-        prepare(right, i, i + HALO + leaves, None)
-        return c
-
-    lax.fori_loop(0, HALO, halo, 0)
-
-    def middle(p, c):
-        for j in range(2):
-            i = p * 2 + j
-            tgt2[p, j * 64 : j * 64 + 64, :] = prepare(own, i, i + HALO, j)
-        return c
-
-    lax.fori_loop(0, leaves // 2, middle, 0)
+    def halo(g, c):
+        for j in range(4):
+            i = g * 4 + j
+            prepare(left, i, i, None)
+            prepare(right, i, i + HALO + leaves, None)
+        return c
+
+    lax.fori_loop(0, HALO // 4, halo, 0)
+
+    def middle(g, c):
+        for j in range(8):
+            i = g * 8 + j
+            half = j % 2
+            tgt2[g * 4 + j // 2, half * 64 : half * 64 + 64, :] = prepare(
+                own, i, i + HALO, half
+            )
+        return c
+
+    lax.fori_loop(0, leaves // 8, middle, 0)
     src[total] = jnp.zeros(src.shape[1:], bf16)
     xw[total] = jnp.zeros(xw.shape[1:], bf16)
     src_lo[total] = jnp.zeros(src_lo.shape[1:], bf16)
@@ -177,21 +185,27 @@
     def near_leaf(l, c):
         target = tgt[l]
 
-        def step(t, acc):
-            tiles, values = [], []
-            for u in range(NEAR_STEP):
-                m = near_ids[l * near_width + t * NEAR_STEP + u]
-                k = profile(jnp.dot(src[m], target, preferred_element_type=f32))
-                hi = k.astype(bf16)
-                tiles += [hi, (k - hi.astype(f32)).astype(bf16)]
-                values.append(xw[m])
-            return acc + jnp.dot(
-                jnp.concatenate(values, axis=1),
-                jnp.concatenate(tiles, axis=0),
-                preferred_element_type=f32,
-            )
-
-        acc = lax.fori_loop(0, near_trips[l], step, jnp.zeros((64, P_SIZE), f32))
+        def steps(count):
+            def run():
+                tiles, values = [], []
+                for u in range(count):
+                    m = near_ids[l * near_width + u]
+                    k = profile(jnp.dot(src[m], target, preferred_element_type=f32))
+                    hi = k.astype(bf16)
+                    tiles += [hi, (k - hi.astype(f32)).astype(bf16)]
+                    values.append(xw[m])
+                return jnp.dot(
+                    jnp.concatenate(values, axis=1),
+                    jnp.concatenate(tiles, axis=0),
+                    preferred_element_type=f32,
+                )
+
+            return run
+
+        acc = lax.switch(
+            jnp.maximum(near_trips[l], 1) - 1,
+            [steps(n) for n in range(NEAR_STEP, near_width + 1, NEAR_STEP)],
+        )
         near_out[l] = (acc[0:32] + acc[32:64]) * near_factor
         return c
 
@@ -200,25 +214,30 @@
     def far_pair(p, c):
         target = tgt2[p]
 
-        def step(t, acc):
-            tiles, values = [], []
-            for u in range(FAR_STEP):
-                at = t * FAR_STEP + u
-                a = far_ids[2 * p * far_width + at]
-                b = far_ids[(2 * p + 1) * far_width + at]
-                k = profile(
-                    jnp.dot(src_lo[a] + src_hi[b], target, preferred_element_type=f32)
+        def steps(count):
+            def run():
+                tiles, values = [], []
+                for at in range(count):
+                    a = far_ids[2 * p * far_width + at]
+                    b = far_ids[(2 * p + 1) * far_width + at]
+                    k = profile(
+                        jnp.dot(src_lo[a] + src_hi[b], target, preferred_element_type=f32)
+                    )
+                    hi = k.astype(bf16)
+                    tiles += [hi, (k - hi.astype(f32)).astype(bf16)]
+                    values.append(jnp.concatenate([qw[a], qw[b]], axis=0))
+                return jnp.dot(
+                    jnp.concatenate(values, axis=1),
+                    jnp.concatenate(tiles, axis=0),
+                    preferred_element_type=f32,
                 )
-                hi = k.astype(bf16)
-                tiles += [hi, (k - hi.astype(f32)).astype(bf16)]
-                values.append(jnp.concatenate([qw[a], qw[b]], axis=0))
-            return acc + jnp.dot(
-                jnp.concatenate(values, axis=1),
-                jnp.concatenate(tiles, axis=0),
-                preferred_element_type=f32,
-            )
-
-        acc = lax.fori_loop(0, far_trips[p], step, jnp.zeros((128, P_SIZE), f32))
+
+            return run
+
+        acc = lax.switch(
+            jnp.maximum(far_trips[p], 1) - 1,
+            [steps(n) for n in range(FAR_STEP, far_width + 1, FAR_STEP)],
+        )
         low = lax.broadcasted_iota(jnp.int32, (32, P_SIZE), 1) < 64
         far_out[p] = (
             jnp.where(low, acc[0:32] + acc[32:64], acc[64:96] + acc[96:128]) * far_factor
@@ -263,7 +282,14 @@
         term = hdot(gathered[m, 0:32, :], tile(source, target))
         return acc + jnp.where(entry >= 0, term, 0.0)
 
-    z2 = lax.fori_loop(0, sub_width, sub_term, jnp.zeros(gathered[0, 0:32, :].shape, f32))
+    many = 4 if sub_width % 4 == 0 else 1
+
+    def sub_terms(g, acc):
+        for j in range(many):
+            acc = sub_term(g * many + j, acc)
+        return acc
+
+    z2 = lax.fori_loop(0, sub_width // many, sub_terms, jnp.zeros(gathered[0, 0:32, :].shape, f32))
     g_own = group_skel[group]
     g_centre = g_own[:, 0:1]
     g_target = centred(g_own, g_centre)[1]
@@ -275,7 +301,9 @@
         source = centred(group_skel[h], g_centre)[0]
         return acc + jnp.where(h != group, hdot(q3, tile(source, g_target)), 0.0)
 
-    z3 = lax.fori_loop(0, groups, group_term, jnp.zeros(z2.shape, f32))
+    z3 = jnp.zeros(z2.shape, f32)
+    for h in range(groups):
+        z3 = group_term(h, z3)
     l2 = z2 * f2 + hdot_nt(z3 * f3, sub_tr[0])
 
     def box_level(b, c):
@@ -289,37 +317,45 @@
             source = centred(box_skel[m], b_centre)[0]
             return acc + jnp.where(entry >= 0, hdot(q1[m], tile(source, b_target)), 0.0)
 
-        z1 = lax.fori_loop(0, box_width, box_term, jnp.zeros((32, P_SIZE), f32))
+        z1 = jnp.zeros((32, P_SIZE), f32)
+        for j in range(box_width):
+            z1 = box_term(j, z1)
         l1s[b] = z1 * f1 + hdot_nt(l2, box_tr[b])
         return c
 
-    lax.fori_loop(0, boxes, box_level, 0)
+    def box_pair(g, c):
+        for j in range(2):
+            box_level(2 * g + j, c)
+        return c
+
+    lax.fori_loop(0, boxes // 2, box_pair, 0)
 
     pad[...] = jnp.zeros_like(pad)
 
-    def down(p, c):
-        l1 = l1s[p // (CH // 2)]
-        z = far[p]
-        for j in range(2):
-            i = 2 * p + j
-            l0 = z[:, 64 * j : 64 * j + 64] + hdot_nt(l1, leaf_tr[i])
-            y = near[i] + hdot(l0, basis[i])
-            pad[j, 0:32, :] = y
-            turned = pad[j].T
-            pad[2 + j] = turned
-            base = i * P_SIZE
+    def down(b, c):
+        l1 = l1s[b]
+        for j in range(CH):
+            i = b * CH + j
+            half = 64 * (j % 2)
+            l0 = far[b * (CH // 2) + j // 2, :, half : half + 64] + hdot_nt(l1, leaf_tr[i])
+            pad[j, 0:32, :] = near[i] + hdot(l0, basis[i])
+        for j in range(CH):
+            pad[CH + j] = pad[j].T
+        for j in range(CH):
+            base = (b * CH + j) * P_SIZE
             for k in range(P_SIZE):
-                rows[pl.ds(morton[base + k], 1), :] = pad[2 + j, k : k + 1, :]
-        return c
-
-    lax.fori_loop(0, leaves // 2, down, 0)
-
-    def flip(i, c):
-        at = pl.ds(pl.multiple_of(i * P_SIZE, P_SIZE), P_SIZE)
-        out[:, at] = rows[at, :].T[0:32]
-        return c
-
-    lax.fori_loop(0, leaves, flip, 0)
+                rows[pl.ds(morton[base + k], 1), :] = pad[CH + j, k : k + 1, :]
+        return c
+
+    lax.fori_loop(0, boxes, down, 0)
+
+    def flip(g, c):
+        for j in range(4):
+            at = pl.ds(pl.multiple_of((4 * g + j) * P_SIZE, P_SIZE), P_SIZE)
+            out[:, at] = rows[at, :].T[0:32]
+        return c
+
+    lax.fori_loop(0, leaves // 4, flip, 0)
 
 
 VMEM = pl.BlockSpec(memory_space=pltpu.VMEM)
@@ -365,8 +401,8 @@
         out_specs=(VMEM,) * 4,
         scratch_shapes=[
             pltpu.VMEM((count, P_SIZE), f32),
-            pltpu.VMEM((P_SIZE, P_SIZE), f32),
-            pltpu.VMEM((2, P_SIZE, P_SIZE), f32),
+            pltpu.VMEM((4, P_SIZE, P_SIZE), f32),
+            pltpu.VMEM((CH, P_SIZE, P_SIZE), f32),
         ],
         compiler_params=params,
         name="arrange",
@@ -430,7 +466,7 @@
         out_specs=VMEM,
         scratch_shapes=[
             pltpu.VMEM((count, P_SIZE), f32),
-            pltpu.VMEM((4, P_SIZE, P_SIZE), f32),
+            pltpu.VMEM((2 * CH, P_SIZE, P_SIZE), f32),
             pltpu.VMEM((boxes, nv, P_SIZE), f32),
         ],
         compiler_params=params,

time: 427 us -> 209 us (0.49)
  Pallas kernels: 372 us -> 156 us
    pallas_call x1, Pallas kernels: 274 us -> 92.1 us  [body(): pl.pallas_call(functools.partial(couple_kernel, near_width=near_width, fa...]
    pallas_call x1, Pallas kernels: 60.8 us -> 43.6 us  [body(): pl.pallas_call(functools.partial(finish_kernel, subs=subs, groups=groups,...]
    pallas_call x1, Pallas kernels: 36.8 us -> 20.7 us  [body(): pl.pallas_call(arrange_kernel, out_shape=(jax.ShapeDtypeStruct((leaves, 5...]
  transfers between devices with their start and end apart: 3 -> 3, of which waited for: 2 -> 2; matrix products, arithmetic and copies ran while one was open for 2% -> 4% of each run, Pallas kernels for 65% -> 45%
where the time goes in v2:
time: 209 us; the launch traced here: 206 us
  Pallas kernels  156 us (75%)
  waiting for transfers between devices  18.4 us (9%)
  between operations  13.5 us (6%)
  local copies, waits for them, and re-layouts  7.67 us (4%)
  starting transfers between devices  6.69 us (3%)
  other arithmetic  3.64 us (2%)
    pallas_call x1, Pallas kernels, body(): pl.pallas_call(functools.partial(couple_kernel, near_width=near_width, fa...  92.1 us
    pallas_call x1, Pallas kernels, body(): pl.pallas_call(functools.partial(finish_kernel, subs=subs, groups=groups,...  43.6 us
    pallas_call x1, Pallas kernels, body(): pl.pallas_call(arrange_kernel, out_shape=(jax.ShapeDtypeStruct((leaves, 5...  20.7 us
    ppermute x1, waiting for transfers between devices, body(): right = lax.ppermute(geo[:HALO], both, [(i + 1, i) for i in range(ends)])  15.1 us
    ppermute x1, starting transfers between devices, body(): lax.ppermute(geo[leaves - HALO:], both, [(i, i + 1) for i in range(ends)])  4.59 us
  transfers between devices with their start and end apart: 3, of which 2 were waited for; matrix products, arithmetic and copies ran while one was open for 4% of the time, Pallas kernels for 45%

profile of v2, /device:TPU:1, one launch (start us, length us, event | category | flops | bytes accessed | tf_op | source)
XLA Modules:
  0.0 206.3 jit_solution(16680867319419483251)
XLA Ops:
  6.5 0.0 all-gather.3.cloned.1.call-start
  6.5 1.6 copy.23.skel
  8.2 0.7 copy.28
  8.8 0.1 pad.13.clone
  8.9 20.7 %arrange.1 = (f32[64,56,128]{2,1,0:T(8,128)}, f32[8,32,128]{2,1,0:T(8,128)}, f32[32,256]{1,0:T(8,128)}, f32[32,256]{1,0:T(8,128)}) custom-call(s32[8192]{0:T(1024)} %morton.3, f32[3,8192]{1,0:T(4,128)} %points.1, f32[32,8192]{1,0:T(8,128)} %probes.1, f32[64,3,64]{2,1,0:T(4,128)} %copy.23.skel, f32[64,64,128]{2,1,0:T(8,128)} %basis.3, ...), custom_call_target="tpu_custom_call" | custom-call | tf_op jit(solution)/shard_map/arrange/pallas_call | solution.py:392
  29.6 0.0 copy-start
  29.6 0.0 copy-start.3
  29.6 0.0 copy-start.1
  29.6 0.0 copy-start.2
  29.6 1.5 maximum_maximum_fusion
  31.1 0.0 copy-start.4
  31.1 0.0 all-gather.3.cloned.1.call-update
  31.2 1.6 fusion.3
  32.7 4.6 %collective-permute-start = (f32[32,56,128]{2,1,0:T(8,128)S(1)}, f32[32,56,128]{2,1,0:T(8,128)S(1)}, u32[]{:S(2)}, u32[]{:S(2)}) collective-permute-start(f32[32,56,128]{2,1,0:T(8,128)S(1)} %get-tuple-element.18), channel_id=1, source_target_pairs={{0,1},{1,2},{2,3},{3,4},{4,5},{5,6},{6,7},{7,8},{8,9},{9,10},{10,1... | collective-permute-start | bytes 2752520 | tf_op jit(solution)/shard_map/ppermute | solution.py:413
  37.3 2.1 %collective-permute-start.1 = (f32[32,56,128]{2,1,0:T(8,128)S(1)}, f32[32,56,128]{2,1,0:T(8,128)}, u32[]{:S(2)}, u32[]{:S(2)}) collective-permute-start(f32[32,56,128]{2,1,0:T(8,128)S(1)} %get-tuple-element.17), channel_id=1, source_target_pairs={{1,0},{2,1},{3,2},{4,3},{5,4},{6,5},{7,6},{8,7},{9,8},{10,9},{11,1... | collective-permute-start | bytes 2752520 | tf_op jit(solution)/shard_map/ppermute | solution.py:414
  39.5 0.0 copy-done
  39.5 0.1 select_reduce_fusion
  39.6 0.1 copy.21
  39.7 0.7 reshape.26.near_ids
  40.4 0.0 copy-done.3
  40.4 0.1 select_reduce_fusion.1
  40.5 0.1 copy.22
  40.6 0.7 reshape.27.far_ids
  41.3 0.1 sub.46
  41.4 0.0 copy-done.1
  41.4 0.6 pad.8.box_skel
  42.0 0.0 copy-done.2
  42.0 0.6 pad.9.group_skel
  42.6 0.0 copy-done.4
  42.6 0.1 copy.20
  42.7 0.7 reshape.24.box_far
  43.4 0.7 pad_add_fusion.place
  44.1 0.7 fusion.1.far_trips
  44.7 0.6 and_select_fusion.near_trips
  45.3 3.3 %collective-permute-done.left = f32[32,56,128]{2,1,0:T(8,128)S(1)} collective-permute-done((f32[32,56,128]{2,1,0:T(8,128)S(1)}, f32[32,56,128]{2,1,0:T(8,128)S(1)}, u32[]{:S(2)}, u32[]{:S(2)}) %collective-permute-start) | collective-permute-done | bytes 917536 | tf_op jit(solution)/shard_map/ppermute | solution.py:413
  48.6 0.0 copy-start.5
  48.6 15.1 %collective-permute-done.1.right = f32[32,56,128]{2,1,0:T(8,128)} collective-permute-done((f32[32,56,128]{2,1,0:T(8,128)S(1)}, f32[32,56,128]{2,1,0:T(8,128)}, u32[]{:S(2)}, u32[]{:S(2)}) %collective-permute-start.1) | collective-permute-done | bytes 917536 | tf_op jit(solution)/shard_map/ppermute | solution.py:414
  63.8 0.0 copy-done.5
  63.8 92.1 %couple.1 = (f32[64,32,128]{2,1,0:T(8,128)}, f32[32,32,128]{2,1,0:T(8,128)}) custom-call(s32[1728]{0:T(1024)} %reshape.26.near_ids, s32[64]{0:T(128)} %and_select_fusion.near_trips, s32[1536]{0:T(1024)} %reshape.27.far_ids, s32[32]{0:T(128)} %fusion.1.far_trips, f32[32,56,128]{2,1,0:T(8,128)} %copy-done.5, f32[64,56,128]{2,1,0:T(8,128)} %get-tuple-element.11.own, ...), custom_call_target="tpu_custom_call" | custom-call | flops 20000000000 | bytes 10000000 | tf_op jit(solution)/shard_map/couple/pallas_call | solution.py:424
  155.9 0.0 all-gather.3.cloned.1.call-done
  155.9 43.6 %finish.1 = f32[32,8192]{1,0:T(8,128)} custom-call(s32[8192]{0:T(1024)} %morton.3, s32[32]{0:T(128)} %reshape.24.box_far, s32[4]{0:T(128)} %bitcast.9, s32[2]{0:T(128)} %pad_add_fusion.place, f32[64,32,128]{2,1,0:T(8,128)} %get-tuple-element.12.near, f32[32,32,128]{2,1,0:T(8,128)} %get-tuple-element.13.far, f32[8,32,128]{2,1,0:T(8,128)} %get-tuple-element.14.q1, ...), custom_call_target="tpu_custom_call" | custom-call | tf_op jit(solution)/shard_map/finish/pallas_call | solution.py:453
  (6 shorter events, 0.0 us)
Async XLA Ops:
  6.5 149.3 %all-gather.3.cloned.1.call-start = ((), (), s32[]{:S(2)}) async-start(), calls=%async_computation | async-start | bytes 2433024 | tf_op jit(solution)/shard_map/all_gather | solution.py:418
  29.6 9.9 %copy-start = (s32[64,27]{0,1:T(8,128)S(1)}, s32[64,27]{0,1:T(8,128)}, u32[]{:S(2)}) copy-start(s32[64,27]{0,1:T(8,128)} %param.18) | copy-start | bytes 20740
  29.6 10.8 %copy-start.3 = (s32[64,24]{0,1:T(8,128)S(1)}, s32[64,24]{0,1:T(8,128)}, u32[]{:S(2)}) copy-start(s32[64,24]{0,1:T(8,128)} %param.19) | copy-start | bytes 18436
  29.6 11.8 %copy-start.1 = (f32[8,3,128]{2,0,1:T(8,128)S(1)}, f32[8,3,128]{2,0,1:T(8,128)}, u32[]{:S(2)}) copy-start(f32[8,3,128]{2,0,1:T(8,128)} %param.23) | copy-start | bytes 36868
  29.6 12.4 %copy-start.2 = (f32[4,3,256]{2,0,1:T(4,128)S(1)}, f32[4,3,256]{2,0,1:T(4,128)}, u32[]{:S(2)}) copy-start(f32[4,3,256]{2,0,1:T(4,128)} %param.25) | copy-start | bytes 36868
  31.1 11.5 %copy-start.4 = (s32[8,4]{0,1:T(4,128)S(1)}, s32[8,4]{0,1:T(4,128)}, u32[]{:S(2)}) copy-start(s32[8,4]{0,1:T(4,128)} %param.20) | copy-start | bytes 388
  32.7 15.9 %collective-permute-start = (f32[32,56,128]{2,1,0:T(8,128)S(1)}, f32[32,56,128]{2,1,0:T(8,128)S(1)}, u32[]{:S(2)}, u32[]{:S(2)}) collective-permute-start(f32[32,56,128]{2,1,0:T(8,128)S(1)} %get-tuple-element.18), channel_id=1, source_target_pairs={{0,1},{1,2},{2,3},{3,4},{4,5},{5,6},{6,7},{7,8},{8,9},{9,10},{10,1... | collective-permute-start | bytes 2752520 | tf_op jit(solution)/shard_map/ppermute | solution.py:413
  37.3 26.4 %collective-permute-start.1 = (f32[32,56,128]{2,1,0:T(8,128)S(1)}, f32[32,56,128]{2,1,0:T(8,128)}, u32[]{:S(2)}, u32[]{:S(2)}) collective-permute-start(f32[32,56,128]{2,1,0:T(8,128)S(1)} %get-tuple-element.17), channel_id=1, source_target_pairs={{1,0},{2,1},{3,2},{4,3},{5,4},{6,5},{7,6},{8,7},{9,8},{10,9},{11,1... | collective-permute-start | bytes 2752520 | tf_op jit(solution)/shard_map/ppermute | solution.py:414
  48.6 15.1 %copy-start.5 = (f32[32,56,128]{2,1,0:T(8,128)}, f32[32,56,128]{2,1,0:T(8,128)S(1)}, u32[]{:S(2)}) copy-start(f32[32,56,128]{2,1,0:T(8,128)S(1)} %collective-permute-done.left) | copy-start | bytes 2752516
Sparse Core Ops, SparseCore 0:
  31.3 60.5 all-gather.2
